TPU v7x, 32 devices: a whole 2x2x4 slice. The times are simulated.
32 devices in a mesh: vocab: 4 (over y, x), docs: 8 (over z, core).
Axes of the slice: x: 2, y: 2, z: 4, core: 2. Of those that a mesh axis runs over, the one named last changes fastest.
Arguments:
- hidden: bfloat16 [24, 256, 2048], P('docs', 'vocab'), may hold values from -6 to 6
- w_vocab: bfloat16 [16384, 2048], P(('vocab', 'docs')), may hold values from -0.125 to 0.125
- lengths: int32 [24], P('docs'), may hold values from 1 to 256, as said below
- query_terms: bfloat16 [1024, 16384], P('docs', 'vocab'), may hold values from -0.09375 to 0.09375
- tile_routes: int32 [8, 128, 4], P('docs', 'vocab'), may hold values from 0 to 7, all different within a row; in each aligned block of 32 rows (0 to 31, 32 to 63, ..., all dimensions but the last counted through in order) at most 32 rows name the same one
Outputs:
- doc_terms: bfloat16 [24, 16384], P('docs', 'vocab')
- scores: float32 [1024, 24], P('docs', 'vocab')
Inputs may be any that keep to these rules, and one draw needn't show every extreme that they name: `lengths`: the last passage has 256 tokens. `tile_routes`: each row names 4 different query tiles; among the 32 rows of one device no query tile is named more than 32 times.
All inputs are finite; a program needn't handle non-finite values.
Results may differ from a plain program's by a relative error of at most 0.009.
Values may be sent and summed in bfloat16 or wider, within the bound.
A program may use at most 384 MiB of HBM per device.

v0:
```python
import jax
import jax.numpy as jnp
from jax import lax
from jax.sharding import PartitionSpec as P

saturate = 1.2
length_slope = 0.75


def pooled_rows(passage_rows, weights, lens_here):
    logits = lax.dot_general(
        passage_rows, weights, (((2,), (1,)), ((), ())), preferred_element_type=jnp.float32
    )
    places = lax.broadcasted_iota(jnp.int32, logits.shape, 1)
    activity = jnp.where(
        places < lens_here[:, None, None], jnp.log1p(jnp.maximum(logits, 0.0)), 0.0
    )
    return jnp.sum(activity, axis=1) / lens_here.astype(jnp.float32)[:, None]


def local(hidden, w_vocab, lengths, query_terms, tile_routes):
    members = lax.axis_size("docs")
    local_count = hidden.shape[0]
    lens_all = lax.all_gather(lengths, "docs", axis=0, tiled=True)
    passage_total = lens_all.shape[0]
    average = jnp.sum(lens_all.astype(jnp.float32)) / passage_total
    full_rows = lax.all_gather(hidden, "vocab", axis=1, tiled=True)
    doc_terms = pooled_rows(
        full_rows, lax.all_gather(w_vocab, "docs", axis=0, tiled=True), lengths
    ).astype(jnp.bfloat16)
    weight = doc_terms.astype(jnp.float32)
    denominator = saturate * (
        1.0 - length_slope + length_slope * lengths.astype(jnp.float32) / average
    )
    scaled = (weight * (saturate + 1.0) / (weight + denominator[:, None])).astype(jnp.bfloat16)
    term_count = scaled.shape[1]
    tile_count = term_count // 128
    my_routes = tile_routes[0]
    fanout = my_routes.shape[1]
    capacity = min(tile_count, max(4, 2 * tile_count * fanout // members))
    owners = lax.broadcasted_iota(jnp.int32, (1, 1, members), 2)
    is_listed = jnp.any(my_routes[:, :, None] == owners, axis=1)
    slot_index = jnp.cumsum(is_listed.astype(jnp.int32), axis=0) - 1
    slot_ids = lax.broadcasted_iota(jnp.int32, (1, capacity, 1), 1)
    selector = (is_listed.T[:, None, :] & (slot_index.T[:, None, :] == slot_ids)).astype(
        jnp.bfloat16
    )
    blocks = scaled.reshape(local_count, tile_count, 128)
    outgoing = jnp.einsum(
        "oct,ptk->ocpk", selector, blocks, preferred_element_type=jnp.float32
    ).astype(jnp.bfloat16)
    tile_ids = lax.broadcasted_iota(jnp.float32, (1, 1, tile_count), 2)
    labels = jnp.sum(selector.astype(jnp.float32) * tile_ids, axis=2).astype(jnp.bfloat16)
    arrived, labels_in = (
        lax.all_to_all(outgoing, "docs", split_axis=0, concat_axis=0, tiled=True),
        lax.all_to_all(labels, "docs", split_axis=0, concat_axis=0, tiled=True),
    )
    placing = (labels_in.astype(jnp.float32)[:, :, None] == tile_ids).astype(jnp.bfloat16)
    masked = jnp.einsum(
        "bct,bcpk->bptk", placing, arrived, preferred_element_type=jnp.float32
    ).astype(jnp.bfloat16)
    masked = masked.reshape(passage_total, term_count)
    partial_value = lax.dot_general(
        query_terms, masked, (((1,), (1,)), ((), ())), preferred_element_type=jnp.float32
    )
    scores = lax.psum_scatter(partial_value, "vocab", scatter_dimension=1, tiled=True)
    return (doc_terms, scores)


def solution(mesh):
    return jax.shard_map(
        local,
        mesh=mesh,
        in_specs=(
            P("docs", "vocab", None),
            P(("vocab", "docs"), None),
            P("docs"),
            P("docs", "vocab"),
            P("docs", "vocab", None),
        ),
        out_specs=(P("docs", "vocab"), P("docs", "vocab")),
        check_vma=False,
    )
```

profile of v0, /device:TPU:0, one launch (start us, length us, event | category | flops | bytes accessed | tf_op | source)
XLA Modules:
  0.0 267.1 jit_solution(789445798696794365)
XLA Ops:
  7.2 0.7 all-gather.3.cloned.1.call-update
  8.0 0.7 all-gather.5.cloned.1.call-update
  8.7 0.7 fusion.23
  9.6 0.1 multiply_reduce_fusion
  9.7 0.6 copy.19
  10.3 6.3 %all-to-all-start.1 = ((bf16[8,1,32]{2,1,0:T(2,128)(2,1)}), bf16[8,1,32]{2,1,0:T(2,128)(2,1)S(1)}, u32[]{:S(2)}, u32[]{:S(2)}) async-start(bf16[8,1,32]{2,1,0:T(2,128)(2,1)} %copy.19), calls=%async_computation.1 | async-start | bytes 8192 | tf_op jit(solution)/shard_map/all_to_all | solution.py:56
  16.6 1.2 dynamic-slice
  18.5 0.9 dynamic-update-slice
  19.4 9.4 %all-reduce = s32[24]{0:T(128)S(1)} all-reduce(s32[24]{0:T(128)S(1)} %dynamic-update-slice), channel_id=1, replica_groups=mesh['vocab'=4,'docs'=8] {'docs'}, use_global_device_ids=true, to_apply=%add | all-reduce | flops 24 | bytes 192
  28.8 0.6 convert_reduce_fusion
  30.0 0.7 add_multiply_fusion
  30.7 0.7 convert_element_type.63
  31.4 1.2 dynamic-slice.1
  33.3 23.3 %all-gather.3.cloned.1.call-done = bf16[3,256,2048]{2,1,0:T(8,128)(2,1)} async-done(((bf16[3,64,2048]{2,1,0:T(8,128)(2,1)}), bf16[3,256,2048]{2,1,0:T(8,128)(2,1)}) %all-gather.3.cloned.1.call-update) | async-done | bytes 3145744 | tf_op jit(solution)/shard_map/all_gather | solution.py:27
  56.6 152.7 %all-gather.5.cloned.1.call-done = bf16[4096,2048]{1,0:T(8,128)(2,1)} async-done(((bf16[512,2048]{1,0:T(8,128)(2,1)}), bf16[4096,2048]{1,0:T(8,128)(2,1)}) %all-gather.5.cloned.1.call-update) | async-done | bytes 16777232 | tf_op jit(solution)/shard_map/all_gather | solution.py:29
  209.3 21.2 %select_reduce_fusion = f32[3,4096]{1,0:T(4,128)S(1)} fusion(bf16[3,256,2048]{2,1,0:T(8,128)(2,1)} %all-gather.3.cloned.1.call-done, bf16[4096,2048]{1,0:T(8,128)(2,1)} %all-gather.5.cloned.1.call-done, s32[3]{0:T(128)} %param.7), kind=kOutput, calls=%fused_computation.2 | convolution fusion | flops 12897472512 | bytes 19972108 | tf_op jit(solution)/shard_map/dot_general | solution.py:11
  230.5 0.9 convolution_convert_fusion
  231.4 3.4 %all-to-all-start = ((bf16[8,32,3,128]{3,1,2,0:T(8,128)(2,1)}), bf16[8,32,3,128]{3,1,2,0:T(8,128)(2,1)S(1)}, u32[]{:S(2)}, u32[]{:S(2)}) async-start(bf16[8,32,3,128]{3,1,2,0:T(8,128)(2,1)} %convolution_convert_fusion), calls=%async_computation | async-start | bytes 393216 | tf_op jit(solution)/shard_map/all_to_all | solution.py:55
  234.8 0.7 divide_convert_fusion
  235.5 7.6 %all-to-all-done = bf16[8,32,3,128]{3,1,2,0:T(8,128)(2,1)S(1)} async-done(((bf16[8,32,3,128]{3,1,2,0:T(8,128)(2,1)}), bf16[8,32,3,128]{3,1,2,0:T(8,128)(2,1)S(1)}, u32[]{:S(2)}, u32[]{:S(2)}) %all-to-all-start) | async-done | bytes 196640 | tf_op jit(solution)/shard_map/all_to_all | solution.py:55
  243.1 0.2 convolution_convert_fusion.1
  243.3 0.4 convolution_bitcast_fusion
  243.7 16.0 %all-reduce.1 = f32[128,24]{0,1:T(8,128)S(1)} all-reduce(f32[128,24]{0,1:T(8,128)S(1)} %convolution_bitcast_fusion), channel_id=2, replica_groups=mesh['vocab'=4,'docs'=8] {'vocab'}, use_global_device_ids=true, to_apply=%region_5.6.clone | all-reduce | flops 3072 | bytes 24576
  259.6 0.6 constant_dynamic-slice_fusion
  (12 shorter events, 0.3 us)
Async XLA Ops:
  7.2 236.1 %copy-start = (bf16[128,4096]{1,0:T(8,128)(2,1)S(1)}, bf16[128,4096]{1,0:T(8,128)(2,1)}, u32[]{:S(2)}) copy-start(bf16[128,4096]{1,0:T(8,128)(2,1)} %param.8) | copy-start | bytes 3145732
  7.2 49.4 %all-gather.3.cloned.1.call-start = ((), (), s32[]{:S(2)}) async-start(), calls=%async_computation.2 | async-start | bytes 3932160 | tf_op jit(solution)/shard_map/all_gather | solution.py:27
  7.9 201.4 %all-gather.5.cloned.1.call-start = ((), (), s32[]{:S(2)}) async-start(), calls=%async_computation.3 | async-start | bytes 18874368 | tf_op jit(solution)/shard_map/all_gather | solution.py:29
  10.3 22.9 %all-to-all-start.1 = ((bf16[8,1,32]{2,1,0:T(2,128)(2,1)}), bf16[8,1,32]{2,1,0:T(2,128)(2,1)S(1)}, u32[]{:S(2)}, u32[]{:S(2)}) async-start(bf16[8,1,32]{2,1,0:T(2,128)(2,1)} %copy.19), calls=%async_computation.1 | async-start | bytes 8192 | tf_op jit(solution)/shard_map/all_to_all | solution.py:56
  231.4 11.7 %all-to-all-start = ((bf16[8,32,3,128]{3,1,2,0:T(8,128)(2,1)}), bf16[8,32,3,128]{3,1,2,0:T(8,128)(2,1)S(1)}, u32[]{:S(2)}, u32[]{:S(2)}) async-start(bf16[8,32,3,128]{3,1,2,0:T(8,128)(2,1)} %convolution_convert_fusion), calls=%async_computation | async-start | bytes 393216 | tf_op jit(solution)/shard_map/all_to_all | solution.py:55
Sparse Core Ops, SparseCore 0:
  9.9 46.6 all-gather.2
  58.2 151.0 all-gather.4
where the time goes:
time: 267 us
  waiting for transfers between devices  185 us (69%)
  blocking collectives  25.3 us (9%)
  matrix products  22.7 us (9%)
  between operations  16.1 us (6%)
  starting transfers between devices  9.79 us (4%)
  local copies, waits for them, and re-layouts  4.7 us (2%)
  other arithmetic  3.51 us (1%)
    all_gather x1, waiting for transfers between devices, local(): lax.all_gather(w_vocab, 'docs', axis=0, tiled=True)  153 us
    unnamed x2, blocking collectives  25.3 us
    all_gather x1, waiting for transfers between devices, local(): full_rows = lax.all_gather(hidden, 'vocab', axis=1, tiled=True)  23.3 us
    dot_general x1, matrix products, pooled_rows(): lax.dot_general(passage_rows, weights, (((2,), (1,)), ((), ())), preferre...  21.2 us
    all_to_all x1, waiting for transfers between devices, local(): lax.all_to_all(outgoing, 'docs', split_axis=0, concat_axis=0, tiled=True)  7.56 us
    all_to_all x1, starting transfers between devices, local(): lax.all_to_all(labels, 'docs', split_axis=0, concat_axis=0, tiled=True)  6.33 us
  transfers between devices with their start and end apart: 4, of which 3 were waited for; matrix products, arithmetic and copies ran while one was open for 3% of the time, Pallas kernels for 0%

commit v1 on v0

--- a/solution.py
+++ b/solution.py
@@ -1,6 +1,8 @@
 import jax
 import jax.numpy as jnp
 from jax import lax
+from jax.experimental import pallas as pl
+from jax.experimental.pallas import tpu as pltpu
 from jax.sharding import PartitionSpec as P
 
 saturate = 1.2
@@ -67,9 +69,405 @@
     return (doc_terms, scores)
 
 
+CHUNK = 256
+MESH = pl.DeviceIdType.MESH
+
+
+def head_kernel(
+    hidden, weights, queries, meta, doc_out, score_out,
+    rows, terms, query_rows, meta_all, keep, pooled, doc_send, doc_all, masked, part, part_send, part_all,
+    local_sem, xh_s, xh_r, w_s, w_r, up_s, down_s, z_r, y_s, y_r, sib_s, sib_r,
+    meta_s, meta_r, doc_s, doc_r, part_s, part_r,
+):
+    v, d = lax.axis_index("vocab"), lax.axis_index("docs")
+    x, y, z, c = v % 2, v // 2, d // 2, d % 2
+    x_side, y_side = (2 * y + 1 - x, d), (2 * (1 - y) + x, d)
+    x_cross, sibling = (2 * y + 1 - x, 2 * z + 1 - c), (v, 2 * z + 1 - c)
+    above, below = (v, d + 2), (v, d - 2)
+
+    def send(src, dst, s_sem, r_sem, to):
+        return pltpu.make_async_remote_copy(
+            src_ref=src, dst_ref=dst, send_sem=s_sem, recv_sem=r_sem, device_id=to, device_id_type=MESH
+        )
+
+    barrier = pltpu.get_barrier_semaphore()
+
+    @pl.loop(0, 16)
+    def _(i):
+        peer_v, peer_d = 2 * y + i // 8, i % 8
+
+        @pl.when(jnp.logical_or(peer_v != v, peer_d != d))
+        def _():
+            pl.semaphore_signal(barrier, inc=1, device_id=(peer_v, peer_d), device_id_type=MESH)
+
+    for i in range(2):
+        pl.semaphore_signal(barrier, inc=1, device_id=(2 * (1 - y) + i, d), device_id_type=MESH)
+    pl.semaphore_wait(barrier, 17)
+
+    def slot(m, vp):
+        return rows.at[m, pl.ds(pl.multiple_of(vp * 64, 64), 64), :]
+
+    def from_x(j):
+        block = slot(z * 3 + j, v)
+        return send(hidden.at[j], block, xh_s.at[j], xh_r.at[j], x_cross)
+
+    def own_rows(j):
+        return pltpu.make_async_copy(hidden.at[j], slot(z * 3 + j, 2 * y + c), local_sem.at[j])
+
+    def own_terms(h):
+        return pltpu.make_async_copy(
+            weights.at[pl.ds(h * CHUNK, CHUNK), :], terms.at[x * 2 + h], local_sem.at[3 + h]
+        )
+
+    own_queries = pltpu.make_async_copy(queries, query_rows, local_sem.at[5])
+
+    def side_terms(h):
+        return send(weights.at[pl.ds(h * CHUNK, CHUNK), :], terms.at[x * 2 + h], w_s.at[h], w_r.at[h], x_side)
+
+    def side_terms_in(h):
+        return send(weights.at[pl.ds(h * CHUNK, CHUNK), :], terms.at[(1 - x) * 2 + h], w_s.at[h], w_r.at[h], x_side)
+
+    def go_up(m):
+        return send(slot(m, 2 * y + c), slot(m, 2 * y + c), up_s.at[m], z_r.at[m], above)
+
+    def go_down(m):
+        return send(slot(m, 2 * y + c), slot(m, 2 * y + c), down_s.at[m], z_r.at[m], below)
+
+    def go_y(m):
+        return send(slot(m, 2 * y + c), slot(m, 2 * y + c), y_s.at[m], y_r.at[m], y_side)
+
+    def come_y(m):
+        block = slot(m, 2 * (1 - y) + c)
+        return send(block, block, y_s.at[m], y_r.at[m], y_side)
+
+    def go_sibling(m, side):
+        block = slot(m, 2 * side + c)
+        return send(block, block, sib_s.at[m * 2 + side], sib_r.at[m * 2 + side], sibling)
+
+    def come_sibling(m, side):
+        block = slot(m, 2 * side + 1 - c)
+        return send(block, block, sib_s.at[m * 2 + side], sib_r.at[m * 2 + side], sibling)
+
+    straight = c == x
+
+    @pl.when(straight)
+    def _():
+        for j in range(3):
+            own_rows(j).start()
+
+    @pl.when(jnp.logical_not(straight))
+    def _():
+        for j in range(3):
+            from_x(j).start()
+
+    def meta_to(i):
+        peer = (d + i) % 8
+        return send(meta, meta_all.at[d], meta_s.at[i], meta_r.at[d], (v, peer))
+
+    def meta_from(i):
+        peer = (d + i) % 8
+        return send(meta, meta_all.at[peer], meta_s.at[i], meta_r.at[peer], (v, peer))
+
+    @pl.loop(1, 8)
+    def _(i):
+        meta_to(i).start()
+
+    meta_all[d] = meta[...]
+    for h in range(2):
+        own_terms(h).start()
+    own_queries.start()
+    pooled[...] = jnp.zeros_like(pooled)
+
+    for j in range(3):
+        @pl.when(straight)
+        def _():
+            own_rows(j).wait()
+
+        @pl.when(jnp.logical_not(straight))
+        def _():
+            slot_in = slot(z * 3 + j, 2 * y + c)
+            send(hidden.at[j], slot_in, xh_s.at[j], xh_r.at[j], x_cross).wait_recv()
+
+        m = z * 3 + j
+
+        @pl.when(z < 3)
+        def _():
+            go_up(m).start()
+
+        @pl.when(z > 0)
+        def _():
+            go_down(m).start()
+
+        go_y(m).start()
+        go_sibling(m, y).start()
+
+    for h in range(2):
+        own_terms(h).wait()
+
+    @pl.loop(1, 8)
+    def _(i):
+        meta_from(i).wait_recv()
+
+    row_id = lax.broadcasted_iota(jnp.int32, (16, 128), 0)
+    mine = d.astype(jnp.float32)
+    for side in range(2):
+        listed = jnp.zeros((16, 128), jnp.float32)
+        for zp in range(4):
+            routes = meta_all[2 * zp + side][0:4, :]
+            hit = jnp.max(jnp.where(routes == mine, 1.0, 0.0), axis=0, keepdims=True)
+            listed = jnp.where(row_id // 4 == zp, hit, listed)
+        for t in range(32):
+            keep[side, :, t * 128:(t + 1) * 128] = jnp.broadcast_to(listed[:, t:t + 1], (16, 128))
+
+    def order(n):
+        end = jnp.logical_or(z == 0, z == 3)
+        step = n - 3
+        end_z = jnp.where(z == 0, z + step // 3 + 1, z - step // 3 - 1)
+        near = jnp.where(step % 2 == 0, z - 1, z + 1)
+        mid_z = jnp.where(n < 9, near, jnp.where(z == 1, 3, 0))
+        mid_j = jnp.where(n < 9, step // 2, n - 9)
+        zp = jnp.where(n < 3, z, jnp.where(end, end_z, mid_z))
+        j = jnp.where(n < 3, n, jnp.where(end, step % 3, mid_j))
+        return zp, j
+
+    place = lax.broadcasted_iota(jnp.int32, (8, CHUNK), 0).astype(jnp.float32)
+
+    def pool(n, q):
+        zp, j = order(n)
+        m = zp * 3 + j
+        logits = lax.dot_general(
+            rows[m], terms[q], (((1,), (1,)), ((), ())), preferred_element_type=jnp.float32
+        )
+        length = meta_all[2 * zp + x, pl.ds(4 + j, 1), :]
+        length = jnp.concatenate([length] * (CHUNK // 128), axis=1)
+        room = length - place
+        total = jnp.zeros((8, CHUNK), jnp.float32)
+        for g in range(0, 32, 8):
+            parts = [
+                jnp.where(room > float(8 * i), jnp.maximum(logits[8 * i:8 * i + 8, :], 0.0), 0.0)
+                for i in range(g, g + 8)
+            ]
+            while len(parts) > 1:
+                parts = [a + b + a * b for a, b in zip(parts[0::2], parts[1::2])]
+            total = total + jnp.log1p(parts[0])
+        pooled[q, pl.ds(zp * 4 + j, 1), :] = jnp.sum(total, axis=0, keepdims=True) / length
+
+    @pl.loop(0, 12)
+    def _(n):
+        k, j = n // 3 + 1, n % 3
+
+        @pl.when(jnp.logical_and(n < 9, z - k >= 0))
+        def _():
+            m = (z - k) * 3 + j
+            go_up(m).wait_recv()
+
+            @pl.when(z < 3)
+            def _():
+                go_up(m).start()
+
+            go_y(m).start()
+            go_sibling(m, y).start()
+
+        @pl.when(jnp.logical_and(n < 9, z + k <= 3))
+        def _():
+            m = (z + k) * 3 + j
+            go_down(m).wait_recv()
+
+            @pl.when(z > 0)
+            def _():
+                go_down(m).start()
+
+            go_y(m).start()
+            go_sibling(m, y).start()
+
+        zp, jj = order(n)
+        m = zp * 3 + jj
+        come_y(m).wait_recv()
+        go_sibling(m, 1 - y).start()
+
+        @pl.when(n == 0)
+        def _():
+            for h in range(2):
+                side_terms(h).start()
+
+        come_sibling(m, 0).wait_recv()
+        come_sibling(m, 1).wait_recv()
+
+        for h, first in ((0, 6), (1, 10)):
+            @pl.when(n == first)
+            def _():
+                side_terms_in(h).wait_recv()
+
+        @pl.loop(0, 4)
+        def _(i):
+            first = jnp.where(i == 2, 6, jnp.where(i == 3, 10, 0))
+            start = jnp.where(n == first, 0, n)
+            stop = jnp.where(n >= first, n + 1, start)
+            q = jnp.where(i < 2, x * 2 + i, (1 - x) * 2 + i - 2)
+
+            def step(at, carry):
+                pool(at, q)
+                return carry
+
+            lax.fori_loop(start, stop, step, 0)
+
+    for side in range(2):
+        for h in range(2):
+            doc_send[side, :, h * CHUNK:(h + 1) * CHUNK] = pooled[side * 2 + h].astype(jnp.bfloat16)
+
+    def doc_to(i):
+        side, peer = i // 8, i % 8
+        return send(doc_send.at[side], doc_all.at[x, d], doc_s.at[i], doc_r.at[x * 8 + d], (2 * y + side, peer))
+
+    def doc_from(i):
+        side, peer = i // 8, i % 8
+        return send(doc_send.at[side], doc_all.at[side, peer], doc_s.at[i], doc_r.at[i], (2 * y + side, peer))
+
+    def not_me(i):
+        return i != x * 8 + d
+
+    @pl.loop(0, 16)
+    def _(i):
+        @pl.when(not_me(i))
+        def _():
+            doc_to(i).start()
+
+    doc_all[x, d] = doc_send[x]
+
+    length_sum = jnp.zeros((1, 128), jnp.float32)
+    for b in range(8):
+        for j in range(3):
+            length_sum = length_sum + meta_all[b, 4 + j:5 + j, :]
+    average = length_sum / 24.0
+    dens = []
+    for side in range(2):
+        length_of = jnp.zeros((16, 128), jnp.float32)
+        for zp in range(4):
+            for j in range(3):
+                length_of = jnp.where(row_id == zp * 4 + j, meta_all[2 * zp + side, 4 + j:5 + j, :], length_of)
+        den = saturate * (1.0 - length_slope + length_slope * length_of / average)
+        dens.append(jnp.concatenate([den] * 4, axis=1))
+    own_queries.wait()
+
+    @pl.loop(0, 16)
+    def _(i):
+        @pl.when(not_me(i))
+        def _():
+            doc_from(i).wait_recv()
+
+    pick_row = lax.broadcasted_iota(jnp.int32, (8, 16), 0)
+    pick_col = lax.broadcasted_iota(jnp.int32, (8, 16), 1)
+    pick = jnp.where(jnp.logical_and(pick_col == z * 4 + pick_row, pick_row < 3), 1.0, 0.0).astype(jnp.bfloat16)
+    for b in range(8):
+        cols = slice(b * 512, (b + 1) * 512)
+        doc_out[:, cols] = jnp.dot(pick, doc_all[c, b], preferred_element_type=jnp.float32)
+        for side in range(2):
+            weight = doc_all[side, b].astype(jnp.float32)
+            scaled = weight * (saturate + 1.0) / (weight + dens[side])
+            masked[side * 16:side * 16 + 16, cols] = jnp.where(
+                keep[side, :, cols] > 0.5, scaled, 0.0
+            ).astype(jnp.bfloat16)
+
+    part[...] = lax.dot_general(
+        masked[...], query_rows[...], (((1,), (1,)), ((), ())), preferred_element_type=jnp.float32
+    )
+    for zp in range(4):
+        for side in range(2):
+            part_send[zp, side * 4:side * 4 + 4, :] = part[side * 16 + zp * 4:side * 16 + zp * 4 + 4, :]
+
+    def part_to(i):
+        return send(part_send.at[(v + i) % 4], part_all.at[v], part_s.at[i], part_r.at[v], ((v + i) % 4, d))
+
+    def part_from(i):
+        peer = (v + i) % 4
+        return send(part_send.at[peer], part_all.at[peer], part_s.at[i], part_r.at[peer], (peer, d))
+
+    for i in range(1, 4):
+        part_to(i).start()
+    part_all[v] = part_send[v]
+
+    @pl.when(jnp.logical_not(straight))
+    def _():
+        for j in range(3):
+            from_x(j).wait_send()
+
+    for h in range(2):
+        side_terms(h).wait_send()
+
+    @pl.loop(0, 12)
+    def _(m):
+        @pl.when(jnp.logical_and(z < 3, m // 3 <= z))
+        def _():
+            go_up(m).wait_send()
+
+        @pl.when(jnp.logical_and(z > 0, m // 3 >= z))
+        def _():
+            go_down(m).wait_send()
+
+        go_y(m).wait_send()
+        go_sibling(m, 0).wait_send()
+        go_sibling(m, 1).wait_send()
+
+    @pl.loop(1, 8)
+    def _(i):
+        meta_to(i).wait_send()
+
+    @pl.loop(0, 16)
+    def _(i):
+        @pl.when(not_me(i))
+        def _():
+            doc_to(i).wait_send()
+
+    for i in range(1, 4):
+        part_from(i).wait_recv()
+        part_to(i).wait_send()
+    score_out[...] = (part_all[0] + part_all[1]) + (part_all[2] + part_all[3])
+
+
+def local_kernel(hidden, w_vocab, lengths, query_terms, tile_routes):
+    routes = jnp.pad(tile_routes[0].T.astype(jnp.float32), ((0, 0), (0, 96)))
+    lens = jnp.broadcast_to(lengths.astype(jnp.float32)[:, None], (3, 128))
+    meta = jnp.concatenate([routes, lens, jnp.zeros((1, 128), jnp.float32)], axis=0)
+    width = hidden.shape[2]
+    any_space, vmem = pl.BlockSpec(memory_space=pl.ANY), pl.BlockSpec(memory_space=pltpu.VMEM)
+    dma = lambda count: pltpu.SemaphoreType.DMA((count,))
+    docs, scores = pl.pallas_call(
+        head_kernel,
+        out_shape=(
+            jax.ShapeDtypeStruct((8, 4096), jnp.float32),
+            jax.ShapeDtypeStruct((8, 128), jnp.float32),
+        ),
+        in_specs=[any_space, any_space, any_space, vmem],
+        out_specs=(vmem, vmem),
+        scratch_shapes=[
+            pltpu.VMEM((12, 256, width), jnp.bfloat16),
+            pltpu.VMEM((4, CHUNK, width), jnp.bfloat16),
+            pltpu.VMEM((128, 4096), jnp.bfloat16),
+            pltpu.VMEM((8, 8, 128), jnp.float32),
+            pltpu.VMEM((2, 16, 4096), jnp.float32),
+            pltpu.VMEM((4, 16, CHUNK), jnp.float32),
+            pltpu.VMEM((2, 16, 512), jnp.bfloat16),
+            pltpu.VMEM((2, 8, 16, 512), jnp.bfloat16),
+            pltpu.VMEM((32, 4096), jnp.bfloat16),
+            pltpu.VMEM((32, 128), jnp.float32),
+            pltpu.VMEM((4, 8, 128), jnp.float32),
+            pltpu.VMEM((4, 8, 128), jnp.float32),
+            dma(6), dma(3), dma(3), dma(2), dma(2), dma(12), dma(12), dma(12), dma(12), dma(12),
+            dma(24), dma(24), dma(8), dma(8), dma(16), dma(16), dma(4), dma(4),
+        ],
+        compiler_params=pltpu.CompilerParams(
+            collective_id=0, has_side_effects=True, vmem_limit_bytes=40 * 1024 * 1024
+        ),
+    )(hidden, w_vocab, query_terms, meta)
+    doc_terms = docs[:3].astype(jnp.bfloat16)
+    return doc_terms, scores.reshape(2, 4, 128)[:, :3].reshape(6, 128).T
+
+
 def solution(mesh):
+    shape = dict(mesh.shape)
+    body = local_kernel if (shape["vocab"], shape["docs"]) == (4, 8) else local
     return jax.shard_map(
-        local,
+        body,
         mesh=mesh,
         in_specs=(
             P("docs", "vocab", None),

time: 267 us -> 104 us (0.39)
  waiting for transfers between devices: 185 us -> 0 us
  Pallas kernels: 0 us -> 96.4 us
  blocking collectives: 25.3 us -> 0 us
  matrix products: 22.7 us -> 0 us
  between operations: 16.1 us -> 0.64 us
  starting transfers between devices: 9.79 us -> 0 us
    all_gather x2 -> x0, waiting for transfers between devices: 176 us -> none  [the longest x1 153 us: local(): lax.all_gather(w_vocab, 'docs', axis=0, tiled=True)]
    pallas_call x0 -> x1, Pallas kernels: none -> 96.4 us  [local_kernel(): pl.pallas_call(head_kernel, out_shape=(jax.ShapeDtypeStruct((8, 4096), jn...]
    unnamed x2 -> x0, blocking collectives: 25.3 us -> none
    dot_general x4 -> x0, matrix products: 22.7 us -> none  [the longest x1 21.2 us: pooled_rows(): lax.dot_general(passage_rows, weights, (((2,), (1,)), ((), ())), preferre...]
    all_to_all x2 -> x0, starting transfers between devices: 9.72 us -> none  [the longest x1 6.33 us: local(): lax.all_to_all(labels, 'docs', split_axis=0, concat_axis=0, tiled=True)]
    all_to_all x2 -> x0, waiting for transfers between devices: 7.56 us -> none  [the longest x1 7.56 us: local(): lax.all_to_all(outgoing, 'docs', split_axis=0, concat_axis=0, tiled=True)]
  transfers between devices with their start and end apart: 4 -> 0, of which waited for: 3 -> 0; matrix products, arithmetic and copies ran while one was open for 3% -> 0% of each run, Pallas kernels for 0% -> 0%
where the time goes in v1:
time: 104 us
  Pallas kernels  96.4 us (93%)
  local copies, waits for them, and re-layouts  5.32 us (5%)
  other arithmetic  1.42 us (1%)
    pallas_call x1, Pallas kernels, local_kernel(): pl.pallas_call(head_kernel, out_shape=(jax.ShapeDtypeStruct((8, 4096), jn...  96.4 us
    unnamed x6, local copies, waits for them, and re-layouts  3.95 us

profile of v1, /device:TPU:0, one launch (start us, length us, event | category | flops | bytes accessed | tf_op | source)
XLA Modules:
  0.0 103.8 jit_solution(2320720763389665823)
XLA Ops:
  0.6 0.7 convert_element_type.18
  1.3 0.1 pad.6.clone
  1.4 0.1 pad.7.clone
  1.4 0.7 convert_bitcast_fusion
  2.1 0.1 fusion.meta
  2.2 0.0 copy-start
  2.2 1.6 %copy-done = bf16[512,2048]{1,0:T(8,128)(2,1)S(1)} copy-done((bf16[512,2048]{1,0:T(8,128)(2,1)S(1)}, bf16[512,2048]{1,0:T(8,128)(2,1)}, u32[]{:S(2)}) %copy-start) | copy-done | bytes 2097176
  3.8 0.0 copy-start.1
  3.8 1.2 %copy-done.1 = bf16[128,4096]{1,0:T(8,128)(2,1)S(1)} copy-done((bf16[128,4096]{1,0:T(8,128)(2,1)S(1)}, bf16[128,4096]{1,0:T(8,128)(2,1)}, u32[]{:S(2)}) %copy-start.1) | copy-done | bytes 1048600
  5.0 0.0 copy-start.2
  5.0 1.1 %copy-done.2 = bf16[3,64,2048]{2,1,0:T(8,128)(2,1)S(1)} copy-done((bf16[3,64,2048]{2,1,0:T(8,128)(2,1)S(1)}, bf16[3,64,2048]{2,1,0:T(8,128)(2,1)}, u32[]{:S(2)}) %copy-start.2) | copy-done | bytes 786456
  6.1 96.4 %shard_map.68 = (f32[8,4096]{1,0:T(8,128)S(1)}, f32[8,128]{1,0:T(8,128)S(1)}) custom-call(bf16[3,64,2048]{2,1,0:T(8,128)(2,1)S(1)} %copy-done.2, bf16[512,2048]{1,0:T(8,128)(2,1)S(1)} %copy-done, bf16[128,4096]{1,0:T(8,128)(2,1)S(1)} %copy-done.1, f32[8,128]{1,0:T(8,128)S(1)} %fusion.meta), custom_call_target="tpu_custom_call" | custom-call | tf_op jit(solution)/shard_map/pallas_call | solution.py:434
  102.6 0.6 slice.12
  103.2 0.6 reshape.13
Async XLA Ops:
  2.2 1.6 %copy-start = (bf16[512,2048]{1,0:T(8,128)(2,1)S(1)}, bf16[512,2048]{1,0:T(8,128)(2,1)}, u32[]{:S(2)}) copy-start(bf16[512,2048]{1,0:T(8,128)(2,1)} %weights.1) | copy-start | bytes 6291460
  3.8 1.2 %copy-start.1 = (bf16[128,4096]{1,0:T(8,128)(2,1)S(1)}, bf16[128,4096]{1,0:T(8,128)(2,1)}, u32[]{:S(2)}) copy-start(bf16[128,4096]{1,0:T(8,128)(2,1)} %queries.1) | copy-start | bytes 3145732
  5.0 1.1 %copy-start.2 = (bf16[3,64,2048]{2,1,0:T(8,128)(2,1)S(1)}, bf16[3,64,2048]{2,1,0:T(8,128)(2,1)}, u32[]{:S(2)}) copy-start(bf16[3,64,2048]{2,1,0:T(8,128)(2,1)} %hidden.1) | copy-start | bytes 2359300

commit v2 on v1

--- a/solution.py
+++ b/solution.py
@@ -75,14 +75,14 @@
 
 def head_kernel(
     hidden, weights, queries, meta, doc_out, score_out,
-    rows, terms, query_rows, meta_all, keep, pooled, doc_send, doc_all, masked, part, part_send, part_all,
-    local_sem, xh_s, xh_r, w_s, w_r, up_s, down_s, z_r, y_s, y_r, sib_s, sib_r,
-    meta_s, meta_r, doc_s, doc_r, part_s, part_r,
+    rows, terms, query_rows, meta_all, keep, pooled, doc_send, doc_all, masked, part, part_send, part_all, sums_in,
+    local_sem, w_s, w_r, up_s, down_s, z_r, y_s, y_r, sib_s, sib_r,
+    meta_s, meta_r, doc_s, doc_r, part_s, part_r, sum_s, sum_r,
 ):
     v, d = lax.axis_index("vocab"), lax.axis_index("docs")
     x, y, z, c = v % 2, v // 2, d // 2, d % 2
     x_side, y_side = (2 * y + 1 - x, d), (2 * (1 - y) + x, d)
-    x_cross, sibling = (2 * y + 1 - x, 2 * z + 1 - c), (v, 2 * z + 1 - c)
+    sibling = (v, 2 * z + 1 - c)
     above, below = (v, d + 2), (v, d - 2)
 
     def send(src, dst, s_sem, r_sem, to):
@@ -92,27 +92,19 @@
 
     barrier = pltpu.get_barrier_semaphore()
 
-    @pl.loop(0, 16)
-    def _(i):
-        peer_v, peer_d = 2 * y + i // 8, i % 8
-
-        @pl.when(jnp.logical_or(peer_v != v, peer_d != d))
-        def _():
-            pl.semaphore_signal(barrier, inc=1, device_id=(peer_v, peer_d), device_id_type=MESH)
-
-    for i in range(2):
-        pl.semaphore_signal(barrier, inc=1, device_id=(2 * (1 - y) + i, d), device_id_type=MESH)
-    pl.semaphore_wait(barrier, 17)
+    @pl.loop(1, 8)
+    def _(i):
+        pl.semaphore_signal(barrier, inc=1, device_id=(v, (d + i) % 8), device_id_type=MESH)
+
+    for i in range(1, 4):
+        pl.semaphore_signal(barrier, inc=1, device_id=((v + i) % 4, d), device_id_type=MESH)
+    pl.semaphore_wait(barrier, 10)
 
     def slot(m, vp):
         return rows.at[m, pl.ds(pl.multiple_of(vp * 64, 64), 64), :]
 
-    def from_x(j):
-        block = slot(z * 3 + j, v)
-        return send(hidden.at[j], block, xh_s.at[j], xh_r.at[j], x_cross)
-
     def own_rows(j):
-        return pltpu.make_async_copy(hidden.at[j], slot(z * 3 + j, 2 * y + c), local_sem.at[j])
+        return pltpu.make_async_copy(hidden.at[j], slot(z * 3 + j, 2 * c + y), local_sem.at[j])
 
     def own_terms(h):
         return pltpu.make_async_copy(
@@ -128,37 +120,30 @@
         return send(weights.at[pl.ds(h * CHUNK, CHUNK), :], terms.at[(1 - x) * 2 + h], w_s.at[h], w_r.at[h], x_side)
 
     def go_up(m):
-        return send(slot(m, 2 * y + c), slot(m, 2 * y + c), up_s.at[m], z_r.at[m], above)
+        return send(slot(m, 2 * c + y), slot(m, 2 * c + y), up_s.at[m], z_r.at[m], above)
 
     def go_down(m):
-        return send(slot(m, 2 * y + c), slot(m, 2 * y + c), down_s.at[m], z_r.at[m], below)
+        return send(slot(m, 2 * c + y), slot(m, 2 * c + y), down_s.at[m], z_r.at[m], below)
 
     def go_y(m):
-        return send(slot(m, 2 * y + c), slot(m, 2 * y + c), y_s.at[m], y_r.at[m], y_side)
+        return send(slot(m, 2 * c + y), slot(m, 2 * c + y), y_s.at[m], y_r.at[m], y_side)
 
     def come_y(m):
-        block = slot(m, 2 * (1 - y) + c)
+        block = slot(m, 2 * c + 1 - y)
         return send(block, block, y_s.at[m], y_r.at[m], y_side)
 
     def go_sibling(m, side):
-        block = slot(m, 2 * side + c)
+        block = slot(m, 2 * c + side)
         return send(block, block, sib_s.at[m * 2 + side], sib_r.at[m * 2 + side], sibling)
 
     def come_sibling(m, side):
-        block = slot(m, 2 * side + 1 - c)
+        block = slot(m, 2 * (1 - c) + side)
         return send(block, block, sib_s.at[m * 2 + side], sib_r.at[m * 2 + side], sibling)
 
-    straight = c == x
-
-    @pl.when(straight)
-    def _():
-        for j in range(3):
-            own_rows(j).start()
-
-    @pl.when(jnp.logical_not(straight))
-    def _():
-        for j in range(3):
-            from_x(j).start()
+    for j in range(3):
+        own_rows(j).start()
+    for h in range(2):
+        side_terms(h).start()
 
     def meta_to(i):
         peer = (d + i) % 8
@@ -179,15 +164,7 @@
     pooled[...] = jnp.zeros_like(pooled)
 
     for j in range(3):
-        @pl.when(straight)
-        def _():
-            own_rows(j).wait()
-
-        @pl.when(jnp.logical_not(straight))
-        def _():
-            slot_in = slot(z * 3 + j, 2 * y + c)
-            send(hidden.at[j], slot_in, xh_s.at[j], xh_r.at[j], x_cross).wait_recv()
-
+        own_rows(j).wait()
         m = z * 3 + j
 
         @pl.when(z < 3)
@@ -217,7 +194,7 @@
             hit = jnp.max(jnp.where(routes == mine, 1.0, 0.0), axis=0, keepdims=True)
             listed = jnp.where(row_id // 4 == zp, hit, listed)
         for t in range(32):
-            keep[side, :, t * 128:(t + 1) * 128] = jnp.broadcast_to(listed[:, t:t + 1], (16, 128))
+            keep[side * 16:side * 16 + 16, t * 128:(t + 1) * 128] = jnp.broadcast_to(listed[:, t:t + 1], (16, 128))
 
     def order(n):
         end = jnp.logical_or(z == 0, z == 3)
@@ -238,19 +215,24 @@
         logits = lax.dot_general(
             rows[m], terms[q], (((1,), (1,)), ((), ())), preferred_element_type=jnp.float32
         )
-        length = meta_all[2 * zp + x, pl.ds(4 + j, 1), :]
-        length = jnp.concatenate([length] * (CHUNK // 128), axis=1)
-        room = length - place
-        total = jnp.zeros((8, CHUNK), jnp.float32)
-        for g in range(0, 32, 8):
-            parts = [
-                jnp.where(room > float(8 * i), jnp.maximum(logits[8 * i:8 * i + 8, :], 0.0), 0.0)
-                for i in range(g, g + 8)
-            ]
-            while len(parts) > 1:
-                parts = [a + b + a * b for a, b in zip(parts[0::2], parts[1::2])]
-            total = total + jnp.log1p(parts[0])
-        pooled[q, pl.ds(zp * 4 + j, 1), :] = jnp.sum(total, axis=0, keepdims=True) / length
+        for core in range(2):
+            length = meta_all[2 * zp + core, pl.ds(4 + j, 1), :]
+            length = jnp.concatenate([length] * (CHUNK // 128), axis=1)
+            total = jnp.zeros((8, CHUNK), jnp.float32)
+            for side in range(2):
+                room = length - place - (64 * x + 128 * side).astype(jnp.float32)
+                at = 128 * core + 64 * side
+                parts = [
+                    jnp.where(room > float(8 * i), jnp.maximum(logits[at + 8 * i:at + 8 * i + 8, :], 0.0), 0.0)
+                    for i in range(8)
+                ]
+                while len(parts) > 1:
+                    parts = [a + b + a * b for a, b in zip(parts[0::2], parts[1::2])]
+                total = total + jnp.log1p(parts[0])
+            pooled[q, pl.ds(core * 16 + zp * 4 + j, 1), :] = jnp.sum(total, axis=0, keepdims=True)
+
+    def sums_to(h):
+        return send(pooled.at[(1 - x) * 2 + h], sums_in.at[h], sum_s.at[h], sum_r.at[h], x_side)
 
     @pl.loop(0, 12)
     def _(n):
@@ -285,25 +267,20 @@
         come_y(m).wait_recv()
         go_sibling(m, 1 - y).start()
 
-        @pl.when(n == 0)
-        def _():
-            for h in range(2):
-                side_terms(h).start()
-
         come_sibling(m, 0).wait_recv()
         come_sibling(m, 1).wait_recv()
 
-        for h, first in ((0, 6), (1, 10)):
+        for h, first in ((0, 5), (1, 9)):
             @pl.when(n == first)
             def _():
                 side_terms_in(h).wait_recv()
 
         @pl.loop(0, 4)
         def _(i):
-            first = jnp.where(i == 2, 6, jnp.where(i == 3, 10, 0))
+            first = jnp.where(i == 0, 5, jnp.where(i == 1, 9, 0))
             start = jnp.where(n == first, 0, n)
             stop = jnp.where(n >= first, n + 1, start)
-            q = jnp.where(i < 2, x * 2 + i, (1 - x) * 2 + i - 2)
+            q = jnp.where(i < 2, (1 - x) * 2 + i, x * 2 + i - 2)
 
             def step(at, carry):
                 pool(at, q)
@@ -311,62 +288,57 @@
 
             lax.fori_loop(start, stop, step, 0)
 
-    for side in range(2):
-        for h in range(2):
-            doc_send[side, :, h * CHUNK:(h + 1) * CHUNK] = pooled[side * 2 + h].astype(jnp.bfloat16)
+            @pl.when(jnp.logical_and(n == 11, i < 2))
+            def _():
+                sums_to(i).start()
+
+    row_32 = lax.broadcasted_iota(jnp.int32, (32, 128), 0)
+    length_of = jnp.ones((32, 128), jnp.float32)
+    for b in range(8):
+        for j in range(3):
+            length_of = jnp.where(row_32 == b % 2 * 16 + b // 2 * 4 + j, meta_all[b, 4 + j:5 + j, :], length_of)
+    length_wide = jnp.concatenate([length_of] * (CHUNK // 128), axis=1)
+    for h in range(2):
+        sums_to(h).wait_recv()
+        total = pooled[x * 2 + h] + sums_in[h]
+        doc_send[:, h * CHUNK:(h + 1) * CHUNK] = (total / length_wide).astype(jnp.bfloat16)
 
     def doc_to(i):
-        side, peer = i // 8, i % 8
-        return send(doc_send.at[side], doc_all.at[x, d], doc_s.at[i], doc_r.at[x * 8 + d], (2 * y + side, peer))
+        return send(doc_send, doc_all.at[d], doc_s.at[i], doc_r.at[d], (v, (d + i) % 8))
 
     def doc_from(i):
-        side, peer = i // 8, i % 8
-        return send(doc_send.at[side], doc_all.at[side, peer], doc_s.at[i], doc_r.at[i], (2 * y + side, peer))
-
-    def not_me(i):
-        return i != x * 8 + d
-
-    @pl.loop(0, 16)
-    def _(i):
-        @pl.when(not_me(i))
-        def _():
-            doc_to(i).start()
-
-    doc_all[x, d] = doc_send[x]
+        peer = (d + i) % 8
+        return send(doc_send, doc_all.at[peer], doc_s.at[i], doc_r.at[peer], (v, peer))
+
+    @pl.loop(1, 8)
+    def _(i):
+        doc_to(i).start()
+
+    doc_all[d] = doc_send[...]
 
     length_sum = jnp.zeros((1, 128), jnp.float32)
     for b in range(8):
         for j in range(3):
             length_sum = length_sum + meta_all[b, 4 + j:5 + j, :]
     average = length_sum / 24.0
-    dens = []
-    for side in range(2):
-        length_of = jnp.zeros((16, 128), jnp.float32)
-        for zp in range(4):
-            for j in range(3):
-                length_of = jnp.where(row_id == zp * 4 + j, meta_all[2 * zp + side, 4 + j:5 + j, :], length_of)
-        den = saturate * (1.0 - length_slope + length_slope * length_of / average)
-        dens.append(jnp.concatenate([den] * 4, axis=1))
+    den = saturate * (1.0 - length_slope + length_slope * length_of / average)
+    den = jnp.concatenate([den] * 4, axis=1)
     own_queries.wait()
 
-    @pl.loop(0, 16)
-    def _(i):
-        @pl.when(not_me(i))
-        def _():
-            doc_from(i).wait_recv()
-
-    pick_row = lax.broadcasted_iota(jnp.int32, (8, 16), 0)
-    pick_col = lax.broadcasted_iota(jnp.int32, (8, 16), 1)
-    pick = jnp.where(jnp.logical_and(pick_col == z * 4 + pick_row, pick_row < 3), 1.0, 0.0).astype(jnp.bfloat16)
+    @pl.loop(1, 8)
+    def _(i):
+        doc_from(i).wait_recv()
+
+    pick_row = lax.broadcasted_iota(jnp.int32, (8, 32), 0)
+    pick_col = lax.broadcasted_iota(jnp.int32, (8, 32), 1)
+    pick = jnp.logical_and(pick_col == c * 16 + z * 4 + pick_row, pick_row < 3)
+    pick = jnp.where(pick, 1.0, 0.0).astype(jnp.bfloat16)
     for b in range(8):
         cols = slice(b * 512, (b + 1) * 512)
-        doc_out[:, cols] = jnp.dot(pick, doc_all[c, b], preferred_element_type=jnp.float32)
-        for side in range(2):
-            weight = doc_all[side, b].astype(jnp.float32)
-            scaled = weight * (saturate + 1.0) / (weight + dens[side])
-            masked[side * 16:side * 16 + 16, cols] = jnp.where(
-                keep[side, :, cols] > 0.5, scaled, 0.0
-            ).astype(jnp.bfloat16)
+        doc_out[:, cols] = jnp.dot(pick, doc_all[b], preferred_element_type=jnp.float32)
+        weight = doc_all[b].astype(jnp.float32)
+        scaled = weight * (saturate + 1.0) / (weight + den)
+        masked[:, cols] = jnp.where(keep[:, cols] > 0.5, scaled, 0.0).astype(jnp.bfloat16)
 
     part[...] = lax.dot_general(
         masked[...], query_rows[...], (((1,), (1,)), ((), ())), preferred_element_type=jnp.float32
@@ -386,13 +358,9 @@
         part_to(i).start()
     part_all[v] = part_send[v]
 
-    @pl.when(jnp.logical_not(straight))
-    def _():
-        for j in range(3):
-            from_x(j).wait_send()
-
     for h in range(2):
         side_terms(h).wait_send()
+        sums_to(h).wait_send()
 
     @pl.loop(0, 12)
     def _(m):
@@ -412,11 +380,9 @@
     def _(i):
         meta_to(i).wait_send()
 
-    @pl.loop(0, 16)
-    def _(i):
-        @pl.when(not_me(i))
-        def _():
-            doc_to(i).wait_send()
+    @pl.loop(1, 8)
+    def _(i):
+        doc_to(i).wait_send()
 
     for i in range(1, 4):
         part_from(i).wait_recv()
@@ -444,19 +410,20 @@
             pltpu.VMEM((4, CHUNK, width), jnp.bfloat16),
             pltpu.VMEM((128, 4096), jnp.bfloat16),
             pltpu.VMEM((8, 8, 128), jnp.float32),
-            pltpu.VMEM((2, 16, 4096), jnp.float32),
-            pltpu.VMEM((4, 16, CHUNK), jnp.float32),
-            pltpu.VMEM((2, 16, 512), jnp.bfloat16),
-            pltpu.VMEM((2, 8, 16, 512), jnp.bfloat16),
+            pltpu.VMEM((32, 4096), jnp.float32),
+            pltpu.VMEM((4, 32, CHUNK), jnp.float32),
+            pltpu.VMEM((32, 512), jnp.bfloat16),
+            pltpu.VMEM((8, 32, 512), jnp.bfloat16),
             pltpu.VMEM((32, 4096), jnp.bfloat16),
             pltpu.VMEM((32, 128), jnp.float32),
             pltpu.VMEM((4, 8, 128), jnp.float32),
             pltpu.VMEM((4, 8, 128), jnp.float32),
-            dma(6), dma(3), dma(3), dma(2), dma(2), dma(12), dma(12), dma(12), dma(12), dma(12),
-            dma(24), dma(24), dma(8), dma(8), dma(16), dma(16), dma(4), dma(4),
+            pltpu.VMEM((2, 32, CHUNK), jnp.float32),
+            dma(6), dma(2), dma(2), dma(12), dma(12), dma(12), dma(12), dma(12), dma(24), dma(24),
+            dma(8), dma(8), dma(8), dma(8), dma(4), dma(4), dma(2), dma(2),
         ],
         compiler_params=pltpu.CompilerParams(
-            collective_id=0, has_side_effects=True, vmem_limit_bytes=40 * 1024 * 1024
+            collective_id=0, has_side_effects=True, vmem_limit_bytes=60 * 1024 * 1024
         ),
     )(hidden, w_vocab, query_terms, meta)
     doc_terms = docs[:3].astype(jnp.bfloat16)

time: 104 us -> 98 us (0.942)
  Pallas kernels: 96.4 us -> 91.8 us
  local copies, waits for them, and re-layouts: 5.32 us -> 2.96 us
    pallas_call x1, Pallas kernels: 96.4 us -> 91.8 us  [local_kernel(): pl.pallas_call(head_kernel, out_shape=(jax.ShapeDtypeStruct((8, 4096), jn...]
    unnamed x6 -> x0, local copies, waits for them, and re-layouts: 3.95 us -> none
where the time goes in v2:
time: 98 us; the launch traced here: 97.4 us
  Pallas kernels  91.8 us (94%)
  local copies, waits for them, and re-layouts  2.96 us (3%)
  other arithmetic  2.01 us (2%)
    pallas_call x1, Pallas kernels, local_kernel(): pl.pallas_call(head_kernel, out_shape=(jax.ShapeDtypeStruct((8, 4096), jn...  91.8 us

profile of v2, /device:TPU:0, one launch (start us, length us, event | category | flops | bytes accessed | tf_op | source)
XLA Modules:
  0.0 97.4 jit_solution(6391206739285181546)
XLA Ops:
  0.6 0.7 convert_element_type.18
  1.3 0.1 pad.6.clone
  1.4 0.1 pad.7.clone
  1.4 0.7 convert_bitcast_fusion
  2.1 0.7 fusion.meta
  2.8 91.8 %shard_map.68 = (f32[8,4096]{1,0:T(8,128)}, f32[8,128]{1,0:T(8,128)}) custom-call(bf16[3,64,2048]{2,1,0:T(8,128)(2,1)} %hidden.1, bf16[512,2048]{1,0:T(8,128)(2,1)} %weights.1, bf16[128,4096]{1,0:T(8,128)(2,1)} %queries.1, f32[8,128]{1,0:T(8,128)} %fusion.meta), custom_call_target="tpu_custom_call" | custom-call | tf_op jit(solution)/shard_map/pallas_call | solution.py:400
  94.5 1.5 %slice.12 = bf16[3,4096]{1,0:T(4,128)(2,1)} slice(f32[8,4096]{1,0:T(8,128)} %get-tuple-element.4), slice={[0:3], [0:4096]} | slice | bytes 49152 | tf_op jit(solution)/shard_map/slice | solution.py:429
  96.1 1.3 %reshape.13 = f32[6,128]{1,0:T(8,128)} reshape(f32[2,3,128]{2,1,0:T(4,128)} %bitcast.9) | data formatting | bytes 6144 | tf_op jit(solution)/shard_map/reshape | solution.py:430

commit v3 on v2

--- a/solution.py
+++ b/solution.py
@@ -75,7 +75,7 @@
 
 def head_kernel(
     hidden, weights, queries, meta, doc_out, score_out,
-    rows, terms, query_rows, meta_all, keep, pooled, doc_send, doc_all, masked, part, part_send, part_all, sums_in,
+    rows, terms, turned, query_rows, meta_all, keep, pooled, doc_send, doc_all, masked, part, part_send, part_all, sums_in,
     local_sem, w_s, w_r, up_s, down_s, z_r, y_s, y_r, sib_s, sib_r,
     meta_s, meta_r, doc_s, doc_r, part_s, part_r, sum_s, sum_r,
 ):
@@ -119,11 +119,25 @@
     def side_terms_in(h):
         return send(weights.at[pl.ds(h * CHUNK, CHUNK), :], terms.at[(1 - x) * 2 + h], w_s.at[h], w_r.at[h], x_side)
 
-    def go_up(m):
-        return send(slot(m, 2 * c + y), slot(m, 2 * c + y), up_s.at[m], z_r.at[m], above)
-
-    def go_down(m):
-        return send(slot(m, 2 * c + y), slot(m, 2 * c + y), down_s.at[m], z_r.at[m], below)
+    def go_up(m, side):
+        block, at = slot(m, 2 * c + side), m * 2 + side
+        return send(block, block, up_s.at[at], z_r.at[at], above)
+
+    def go_down(m, side):
+        block, at = slot(m, 2 * c + side), m * 2 + side
+        return send(block, block, down_s.at[at], z_r.at[at], below)
+
+    def onward(m, side, up, down):
+        @pl.when(jnp.logical_and(up, z < 3))
+        def _():
+            go_up(m, side).start()
+
+        @pl.when(jnp.logical_and(down, z > 0))
+        def _():
+            go_down(m, side).start()
+
+    def y_first(j):
+        return jnp.logical_and(c == 0, j == 0)
 
     def go_y(m):
         return send(slot(m, 2 * c + y), slot(m, 2 * c + y), y_s.at[m], y_r.at[m], y_side)
@@ -167,19 +181,13 @@
         own_rows(j).wait()
         m = z * 3 + j
 
-        @pl.when(z < 3)
-        def _():
-            go_up(m).start()
-
-        @pl.when(z > 0)
-        def _():
-            go_down(m).start()
-
+        onward(m, y, True, True)
         go_y(m).start()
         go_sibling(m, y).start()
 
     for h in range(2):
         own_terms(h).wait()
+        turned[x * 2 + h] = terms[x * 2 + h].T
 
     @pl.loop(1, 8)
     def _(i):
@@ -213,7 +221,7 @@
         zp, j = order(n)
         m = zp * 3 + j
         logits = lax.dot_general(
-            rows[m], terms[q], (((1,), (1,)), ((), ())), preferred_element_type=jnp.float32
+            rows[m], turned[q], (((1,), (0,)), ((), ())), preferred_element_type=jnp.float32
         )
         for core in range(2):
             length = meta_all[2 * zp + core, pl.ds(4 + j, 1), :]
@@ -234,52 +242,65 @@
     def sums_to(h):
         return send(pooled.at[(1 - x) * 2 + h], sums_in.at[h], sum_s.at[h], sum_r.at[h], x_side)
 
+    def from_z(zp, j, up):
+        m = zp * 3 + j
+        go_up(m, y).wait_recv()
+        onward(m, y, up, not up)
+
+        @pl.when(jnp.logical_not(y_first(j)))
+        def _():
+            go_y(m).start()
+
+        go_sibling(m, y).start()
+
+        @pl.when(jnp.logical_and(c == 0, j == 2))
+        def _():
+            first = zp * 3
+            go_up(first, 1 - y).wait_recv()
+            onward(first, 1 - y, up, not up)
+            go_sibling(first, 1 - y).start()
+
     @pl.loop(0, 12)
     def _(n):
-        k, j = n // 3 + 1, n % 3
-
-        @pl.when(jnp.logical_and(n < 9, z - k >= 0))
-        def _():
-            m = (z - k) * 3 + j
-            go_up(m).wait_recv()
-
-            @pl.when(z < 3)
-            def _():
-                go_up(m).start()
-
-            go_y(m).start()
-            go_sibling(m, y).start()
-
-        @pl.when(jnp.logical_and(n < 9, z + k <= 3))
-        def _():
-            m = (z + k) * 3 + j
-            go_down(m).wait_recv()
-
-            @pl.when(z > 0)
-            def _():
-                go_down(m).start()
-
-            go_y(m).start()
-            go_sibling(m, y).start()
-
         zp, jj = order(n)
         m = zp * 3 + jj
-        come_y(m).wait_recv()
-        go_sibling(m, 1 - y).start()
+
+        @pl.when(jnp.logical_or(jnp.logical_not(y_first(jj)), zp == z))
+        def _():
+            come_y(m).wait_recv()
+
+            @pl.when(y_first(jj))
+            def _():
+                onward(m, 1 - y, True, True)
+
+            go_sibling(m, 1 - y).start()
+
+        k, j = n // 3 + 1, n % 3
+
+        @pl.when(jnp.logical_and(n < 9, z - k >= 0))
+        def _():
+            from_z(z - k, j, True)
+
+        @pl.when(jnp.logical_and(n < 9, z + k <= 3))
+        def _():
+            from_z(z + k, j, False)
 
         come_sibling(m, 0).wait_recv()
         come_sibling(m, 1).wait_recv()
 
-        for h, first in ((0, 5), (1, 9)):
+        for h, first in ((0, 5), (1, 8)):
             @pl.when(n == first)
             def _():
                 side_terms_in(h).wait_recv()
+                turned[(1 - x) * 2 + h] = terms[(1 - x) * 2 + h].T
 
         @pl.loop(0, 4)
         def _(i):
-            first = jnp.where(i == 0, 5, jnp.where(i == 1, 9, 0))
-            start = jnp.where(n == first, 0, n)
-            stop = jnp.where(n >= first, n + 1, start)
+            late = 4 * (n - 8) - (n - 8) // 3
+            start = jnp.where(i == 1, jnp.where(n < 8, n, late), jnp.where(jnp.logical_and(i == 0, n == 5), 0, n))
+            late_stop = jnp.where(n < 8, n, jnp.minimum(4 * (n - 7) - (n - 7) // 3, 12))
+            early_stop = jnp.where(jnp.logical_and(i == 0, n < 5), n, n + 1)
+            stop = jnp.where(i == 1, late_stop, early_stop)
             q = jnp.where(i < 2, (1 - x) * 2 + i, x * 2 + i - 2)
 
             def step(at, carry):
@@ -364,15 +385,21 @@
 
     @pl.loop(0, 12)
     def _(m):
-        @pl.when(jnp.logical_and(z < 3, m // 3 <= z))
-        def _():
-            go_up(m).wait_send()
-
-        @pl.when(jnp.logical_and(z > 0, m // 3 >= z))
-        def _():
-            go_down(m).wait_send()
-
-        go_y(m).wait_send()
+        zp, j = m // 3, m % 3
+        crossed = jnp.logical_and(y_first(j), zp != z)
+        for side, there in ((y, True), (1 - y, y_first(j))):
+            @pl.when(jnp.logical_and(there, jnp.logical_and(z < 3, zp <= z)))
+            def _():
+                go_up(m, side).wait_send()
+
+            @pl.when(jnp.logical_and(there, jnp.logical_and(z > 0, zp >= z)))
+            def _():
+                go_down(m, side).wait_send()
+
+        @pl.when(jnp.logical_not(crossed))
+        def _():
+            go_y(m).wait_send()
+
         go_sibling(m, 0).wait_send()
         go_sibling(m, 1).wait_send()
 
@@ -408,6 +435,7 @@
         scratch_shapes=[
             pltpu.VMEM((12, 256, width), jnp.bfloat16),
             pltpu.VMEM((4, CHUNK, width), jnp.bfloat16),
+            pltpu.VMEM((4, width, CHUNK), jnp.bfloat16),
             pltpu.VMEM((128, 4096), jnp.bfloat16),
             pltpu.VMEM((8, 8, 128), jnp.float32),
             pltpu.VMEM((32, 4096), jnp.float32),
@@ -419,7 +447,7 @@
             pltpu.VMEM((4, 8, 128), jnp.float32),
             pltpu.VMEM((4, 8, 128), jnp.float32),
             pltpu.VMEM((2, 32, CHUNK), jnp.float32),
-            dma(6), dma(2), dma(2), dma(12), dma(12), dma(12), dma(12), dma(12), dma(24), dma(24),
+            dma(6), dma(2), dma(2), dma(24), dma(24), dma(24), dma(12), dma(12), dma(24), dma(24),
             dma(8), dma(8), dma(8), dma(8), dma(4), dma(4), dma(2), dma(2),
         ],
         compiler_params=pltpu.CompilerParams(

time: 98 us -> 100 us (1.020)
  Pallas kernels: 91.8 us -> 94.2 us
    pallas_call x1, Pallas kernels: 91.8 us -> 94.2 us  [local_kernel(): pl.pallas_call(head_kernel, out_shape=(jax.ShapeDtypeStruct((8, 4096), jn...]
where the time goes in v3:
time: 100 us; the launch traced here: 99.8 us
  Pallas kernels  94.2 us (94%)
  local copies, waits for them, and re-layouts  2.96 us (3%)
  other arithmetic  2.01 us (2%)
    pallas_call x1, Pallas kernels, local_kernel(): pl.pallas_call(head_kernel, out_shape=(jax.ShapeDtypeStruct((8, 4096), jn...  94.2 us

profile of v3, /device:TPU:0, one launch (start us, length us, event | category | flops | bytes accessed | tf_op | source)
XLA Modules:
  0.0 99.8 jit_solution(10501423269907047346)
XLA Ops:
  0.6 0.7 convert_element_type.18
  1.3 0.1 pad.6.clone
  1.4 0.1 pad.7.clone
  1.4 0.7 convert_bitcast_fusion
  2.1 0.7 fusion.meta
  2.8 94.2 %shard_map.68 = (f32[8,4096]{1,0:T(8,128)}, f32[8,128]{1,0:T(8,128)}) custom-call(bf16[3,64,2048]{2,1,0:T(8,128)(2,1)} %hidden.1, bf16[512,2048]{1,0:T(8,128)(2,1)} %weights.1, bf16[128,4096]{1,0:T(8,128)(2,1)} %queries.1, f32[8,128]{1,0:T(8,128)} %fusion.meta), custom_call_target="tpu_custom_call" | custom-call | tf_op jit(solution)/shard_map/pallas_call | solution.py:427
  97.0 1.5 %slice.12 = bf16[3,4096]{1,0:T(4,128)(2,1)} slice(f32[8,4096]{1,0:T(8,128)} %get-tuple-element.4), slice={[0:3], [0:4096]} | slice | bytes 49152 | tf_op jit(solution)/shard_map/slice | solution.py:457
  98.5 1.3 %reshape.13 = f32[6,128]{1,0:T(8,128)} reshape(f32[2,3,128]{2,1,0:T(4,128)} %bitcast.9) | data formatting | bytes 6144 | tf_op jit(solution)/shard_map/reshape | solution.py:458

commit v4 on v3

--- a/solution.py
+++ b/solution.py
@@ -127,14 +127,23 @@
         block, at = slot(m, 2 * c + side), m * 2 + side
         return send(block, block, down_s.at[at], z_r.at[at], below)
 
-    def onward(m, side, up, down):
-        @pl.when(jnp.logical_and(up, z < 3))
-        def _():
-            go_up(m, side).start()
-
-        @pl.when(jnp.logical_and(down, z > 0))
-        def _():
-            go_down(m, side).start()
+    items = 4 - c
+
+    def item(at):
+        extra = at % items == 3
+        return jnp.where(extra, 0, (at % items + 1) % 3), jnp.where(extra, 1 - y, y)
+
+    def send_z(at):
+        far = at // items
+        j, side = item(at)
+
+        @pl.when(jnp.logical_and(z < 3, z - far >= 0))
+        def _():
+            go_up((z - far) * 3 + j, side).start()
+
+        @pl.when(jnp.logical_and(z > 0, z + far <= 3))
+        def _():
+            go_down((z + far) * 3 + j, side).start()
 
     def y_first(j):
         return jnp.logical_and(c == 0, j == 0)
@@ -156,8 +165,7 @@
 
     for j in range(3):
         own_rows(j).start()
-    for h in range(2):
-        side_terms(h).start()
+    side_terms(0).start()
 
     def meta_to(i):
         peer = (d + i) % 8
@@ -179,11 +187,11 @@
 
     for j in range(3):
         own_rows(j).wait()
-        m = z * 3 + j
-
-        onward(m, y, True, True)
-        go_y(m).start()
-        go_sibling(m, y).start()
+    for j in range(2):
+        send_z(j)
+        go_y(z * 3 + j).start()
+    for j in range(3):
+        go_sibling(z * 3 + j, y).start()
 
     for h in range(2):
         own_terms(h).wait()
@@ -212,7 +220,7 @@
         mid_z = jnp.where(n < 9, near, jnp.where(z == 1, 3, 0))
         mid_j = jnp.where(n < 9, step // 2, n - 9)
         zp = jnp.where(n < 3, z, jnp.where(end, end_z, mid_z))
-        j = jnp.where(n < 3, n, jnp.where(end, step % 3, mid_j))
+        j = jnp.where(n < 3, n, (jnp.where(end, step % 3, mid_j) + 1) % 3)
         return zp, j
 
     place = lax.broadcasted_iota(jnp.int32, (8, CHUNK), 0).astype(jnp.float32)
@@ -242,64 +250,59 @@
     def sums_to(h):
         return send(pooled.at[(1 - x) * 2 + h], sums_in.at[h], sum_s.at[h], sum_r.at[h], x_side)
 
-    def from_z(zp, j, up):
-        m = zp * 3 + j
-        go_up(m, y).wait_recv()
-        onward(m, y, up, not up)
-
-        @pl.when(jnp.logical_not(y_first(j)))
-        def _():
-            go_y(m).start()
-
-        go_sibling(m, y).start()
-
-        @pl.when(jnp.logical_and(c == 0, j == 2))
-        def _():
-            first = zp * 3
-            go_up(first, 1 - y).wait_recv()
-            onward(first, 1 - y, up, not up)
-            go_sibling(first, 1 - y).start()
+    def crosses(zp, j):
+        return jnp.logical_or(jnp.logical_not(y_first(j)), zp == z)
 
     @pl.loop(0, 12)
     def _(n):
         zp, jj = order(n)
         m = zp * 3 + jj
 
-        @pl.when(jnp.logical_or(jnp.logical_not(y_first(jj)), zp == z))
+        @pl.when(crosses(zp, jj))
         def _():
             come_y(m).wait_recv()
-
-            @pl.when(y_first(jj))
-            def _():
-                onward(m, 1 - y, True, True)
-
             go_sibling(m, 1 - y).start()
 
-        k, j = n // 3 + 1, n % 3
-
-        @pl.when(jnp.logical_and(n < 9, z - k >= 0))
-        def _():
-            from_z(z - k, j, True)
-
-        @pl.when(jnp.logical_and(n < 9, z + k <= 3))
-        def _():
-            from_z(z + k, j, False)
+        far = n // items + 1
+        j, side = item(n)
+
+        @pl.when(z - far >= 0)
+        def _():
+            at = (z - far) * 3 + j
+            go_up(at, side).wait_recv()
+            go_sibling(at, side).start()
+
+        @pl.when(z + far <= 3)
+        def _():
+            at = (z + far) * 3 + j
+            go_down(at, side).wait_recv()
+            go_sibling(at, side).start()
+
+        send_z(n + 2)
+        ahead = n + 1 + c
+        next_z, next_j = order(ahead)
+
+        @pl.when(jnp.logical_and(jnp.logical_and(ahead >= 2, ahead < 12), crosses(next_z, next_j)))
+        def _():
+            go_y(next_z * 3 + next_j).start()
 
         come_sibling(m, 0).wait_recv()
         come_sibling(m, 1).wait_recv()
 
-        for h, first in ((0, 5), (1, 8)):
+        for h, first in ((0, 4), (1, 9)):
             @pl.when(n == first)
             def _():
                 side_terms_in(h).wait_recv()
+                if h == 0:
+                    side_terms(1).start()
                 turned[(1 - x) * 2 + h] = terms[(1 - x) * 2 + h].T
 
         @pl.loop(0, 4)
         def _(i):
-            late = 4 * (n - 8) - (n - 8) // 3
-            start = jnp.where(i == 1, jnp.where(n < 8, n, late), jnp.where(jnp.logical_and(i == 0, n == 5), 0, n))
-            late_stop = jnp.where(n < 8, n, jnp.minimum(4 * (n - 7) - (n - 7) // 3, 12))
-            early_stop = jnp.where(jnp.logical_and(i == 0, n < 5), n, n + 1)
+            late = 5 * (n - 9)
+            start = jnp.where(i == 1, jnp.where(n < 9, n, late), jnp.where(jnp.logical_and(i == 0, n == 4), 0, n))
+            late_stop = jnp.where(n < 9, n, jnp.minimum(late + 5, 12))
+            early_stop = jnp.where(jnp.logical_and(i == 0, n < 4), n, n + 1)
             stop = jnp.where(i == 1, late_stop, early_stop)
             q = jnp.where(i < 2, (1 - x) * 2 + i, x * 2 + i - 2)
 

time: 100 us -> 102 us (1.020)
  Pallas kernels: 94.2 us -> 96.3 us
    pallas_call x1, Pallas kernels: 94.2 us -> 96.3 us  [local_kernel(): pl.pallas_call(head_kernel, out_shape=(jax.ShapeDtypeStruct((8, 4096), jn...]
where the time goes in v4:
time: 102 us
  Pallas kernels  96.3 us (94%)
  local copies, waits for them, and re-layouts  2.96 us (3%)
  other arithmetic  2.01 us (2%)
    pallas_call x1, Pallas kernels, local_kernel(): pl.pallas_call(head_kernel, out_shape=(jax.ShapeDtypeStruct((8, 4096), jn...  96.3 us

profile of v4, /device:TPU:0, one launch (start us, length us, event | category | flops | bytes accessed | tf_op | source)
XLA Modules:
  0.0 101.9 jit_solution(16931935468239154444)
XLA Ops:
  0.6 0.7 convert_element_type.18
  1.3 0.1 pad.6.clone
  1.4 0.1 pad.7.clone
  1.4 0.7 convert_bitcast_fusion
  2.1 0.7 fusion.meta
  2.8 96.3 %shard_map.68 = (f32[8,4096]{1,0:T(8,128)}, f32[8,128]{1,0:T(8,128)}) custom-call(bf16[3,64,2048]{2,1,0:T(8,128)(2,1)} %hidden.1, bf16[512,2048]{1,0:T(8,128)(2,1)} %weights.1, bf16[128,4096]{1,0:T(8,128)(2,1)} %queries.1, f32[8,128]{1,0:T(8,128)} %fusion.meta), custom_call_target="tpu_custom_call" | custom-call | tf_op jit(solution)/shard_map/pallas_call | solution.py:430
  99.1 1.5 %slice.12 = bf16[3,4096]{1,0:T(4,128)(2,1)} slice(f32[8,4096]{1,0:T(8,128)} %get-tuple-element.4), slice={[0:3], [0:4096]} | slice | bytes 49152 | tf_op jit(solution)/shard_map/slice | solution.py:460
  100.7 1.3 %reshape.13 = f32[6,128]{1,0:T(8,128)} reshape(f32[2,3,128]{2,1,0:T(4,128)} %bitcast.9) | data formatting | bytes 6144 | tf_op jit(solution)/shard_map/reshape | solution.py:461

commit v5 on v4

--- a/solution.py
+++ b/solution.py
@@ -279,10 +279,12 @@
             go_sibling(at, side).start()
 
         send_z(n + 2)
-        ahead = n + 1 + c
+        ahead = jnp.where(jnp.logical_and(c == 0, n > 7), n + 1, n + 2)
+        skip = jnp.logical_and(c == 0, n == 7)
         next_z, next_j = order(ahead)
-
-        @pl.when(jnp.logical_and(jnp.logical_and(ahead >= 2, ahead < 12), crosses(next_z, next_j)))
+        crossing = jnp.logical_and(ahead < 12, crosses(next_z, next_j))
+
+        @pl.when(jnp.logical_and(crossing, jnp.logical_not(skip)))
         def _():
             go_y(next_z * 3 + next_j).start()
 

time: 102 us -> 99.6 us (0.976)
  Pallas kernels: 96.3 us -> 93.8 us
    pallas_call x1, Pallas kernels: 96.3 us -> 93.8 us  [local_kernel(): pl.pallas_call(head_kernel, out_shape=(jax.ShapeDtypeStruct((8, 4096), jn...]
where the time goes in v5:
time: 99.6 us; the launch traced here: 99.4 us
  Pallas kernels  93.8 us (94%)
  local copies, waits for them, and re-layouts  2.96 us (3%)
  other arithmetic  2.01 us (2%)
    pallas_call x1, Pallas kernels, local_kernel(): pl.pallas_call(head_kernel, out_shape=(jax.ShapeDtypeStruct((8, 4096), jn...  93.8 us

profile of v5, /device:TPU:0, one launch (start us, length us, event | category | flops | bytes accessed | tf_op | source)
XLA Modules:
  0.0 99.4 jit_solution(11335169798519644604)
XLA Ops:
  0.6 0.7 convert_element_type.18
  1.3 0.1 pad.6.clone
  1.4 0.1 pad.7.clone
  1.4 0.7 convert_bitcast_fusion
  2.1 0.7 fusion.meta
  2.8 93.8 %shard_map.68 = (f32[8,4096]{1,0:T(8,128)}, f32[8,128]{1,0:T(8,128)}) custom-call(bf16[3,64,2048]{2,1,0:T(8,128)(2,1)} %hidden.1, bf16[512,2048]{1,0:T(8,128)(2,1)} %weights.1, bf16[128,4096]{1,0:T(8,128)(2,1)} %queries.1, f32[8,128]{1,0:T(8,128)} %fusion.meta), custom_call_target="tpu_custom_call" | custom-call | tf_op jit(solution)/shard_map/pallas_call | solution.py:432
  96.6 1.5 %slice.12 = bf16[3,4096]{1,0:T(4,128)(2,1)} slice(f32[8,4096]{1,0:T(8,128)} %get-tuple-element.4), slice={[0:3], [0:4096]} | slice | bytes 49152 | tf_op jit(solution)/shard_map/slice | solution.py:462
  98.1 1.3 %reshape.13 = f32[6,128]{1,0:T(8,128)} reshape(f32[2,3,128]{2,1,0:T(4,128)} %bitcast.9) | data formatting | bytes 6144 | tf_op jit(solution)/shard_map/reshape | solution.py:463

commit v6 on v5

--- a/solution.py
+++ b/solution.py
@@ -106,18 +106,11 @@
     def own_rows(j):
         return pltpu.make_async_copy(hidden.at[j], slot(z * 3 + j, 2 * c + y), local_sem.at[j])
 
-    def own_terms(h):
-        return pltpu.make_async_copy(
-            weights.at[pl.ds(h * CHUNK, CHUNK), :], terms.at[x * 2 + h], local_sem.at[3 + h]
-        )
-
-    own_queries = pltpu.make_async_copy(queries, query_rows, local_sem.at[5])
-
-    def side_terms(h):
-        return send(weights.at[pl.ds(h * CHUNK, CHUNK), :], terms.at[x * 2 + h], w_s.at[h], w_r.at[h], x_side)
-
-    def side_terms_in(h):
-        return send(weights.at[pl.ds(h * CHUNK, CHUNK), :], terms.at[(1 - x) * 2 + h], w_s.at[h], w_r.at[h], x_side)
+    own_terms = pltpu.make_async_copy(weights, terms.at[x], local_sem.at[3])
+    own_queries = pltpu.make_async_copy(queries, query_rows, local_sem.at[4])
+
+    side_terms = send(weights, terms.at[x], w_s.at[0], w_r.at[0], x_side)
+    side_terms_in = send(weights, terms.at[1 - x], w_s.at[0], w_r.at[0], x_side)
 
     def go_up(m, side):
         block, at = slot(m, 2 * c + side), m * 2 + side
@@ -165,7 +158,7 @@
 
     for j in range(3):
         own_rows(j).start()
-    side_terms(0).start()
+    side_terms.start()
 
     def meta_to(i):
         peer = (d + i) % 8
@@ -180,8 +173,7 @@
         meta_to(i).start()
 
     meta_all[d] = meta[...]
-    for h in range(2):
-        own_terms(h).start()
+    own_terms.start()
     own_queries.start()
     pooled[...] = jnp.zeros_like(pooled)
 
@@ -193,9 +185,8 @@
     for j in range(3):
         go_sibling(z * 3 + j, y).start()
 
-    for h in range(2):
-        own_terms(h).wait()
-        turned[x * 2 + h] = terms[x * 2 + h].T
+    own_terms.wait()
+    turned[x] = terms[x].T
 
     @pl.loop(1, 8)
     def _(i):
@@ -225,30 +216,29 @@
 
     place = lax.broadcasted_iota(jnp.int32, (8, CHUNK), 0).astype(jnp.float32)
 
-    def pool(n, q):
+    def pool(n, group):
         zp, j = order(n)
         m = zp * 3 + j
-        logits = lax.dot_general(
-            rows[m], turned[q], (((1,), (0,)), ((), ())), preferred_element_type=jnp.float32
-        )
-        for core in range(2):
-            length = meta_all[2 * zp + core, pl.ds(4 + j, 1), :]
-            length = jnp.concatenate([length] * (CHUNK // 128), axis=1)
-            total = jnp.zeros((8, CHUNK), jnp.float32)
-            for side in range(2):
-                room = length - place - (64 * x + 128 * side).astype(jnp.float32)
-                at = 128 * core + 64 * side
-                parts = [
-                    jnp.where(room > float(8 * i), jnp.maximum(logits[at + 8 * i:at + 8 * i + 8, :], 0.0), 0.0)
-                    for i in range(8)
-                ]
-                while len(parts) > 1:
-                    parts = [a + b + a * b for a, b in zip(parts[0::2], parts[1::2])]
-                total = total + jnp.log1p(parts[0])
-            pooled[q, pl.ds(core * 16 + zp * 4 + j, 1), :] = jnp.sum(total, axis=0, keepdims=True)
-
-    def sums_to(h):
-        return send(pooled.at[(1 - x) * 2 + h], sums_in.at[h], sum_s.at[h], sum_r.at[h], x_side)
+        for half in range(0, 512, CHUNK):
+            logits = jnp.dot(rows[m], turned[group, :, half:half + CHUNK], preferred_element_type=jnp.float32)
+            for core in range(2):
+                length = meta_all[2 * zp + core, pl.ds(4 + j, 1), :]
+                length = jnp.concatenate([length] * (CHUNK // 128), axis=1)
+                total = jnp.zeros((8, CHUNK), jnp.float32)
+                for side in range(2):
+                    room = length - place - (64 * x + 128 * side).astype(jnp.float32)
+                    at = 128 * core + 64 * side
+                    parts = [
+                        jnp.where(room > float(8 * i), jnp.maximum(logits[at + 8 * i:at + 8 * i + 8, :], 0.0), 0.0)
+                        for i in range(8)
+                    ]
+                    while len(parts) > 1:
+                        parts = [a + b + a * b for a, b in zip(parts[0::2], parts[1::2])]
+                    total = total + jnp.log1p(parts[0])
+                row = pl.ds(core * 16 + zp * 4 + j, 1)
+                pooled[group, row, half:half + CHUNK] = jnp.sum(total, axis=0, keepdims=True)
+
+    sums_to = send(pooled.at[1 - x], sums_in, sum_s.at[0], sum_r.at[0], x_side)
 
     def crosses(zp, j):
         return jnp.logical_or(jnp.logical_not(y_first(j)), zp == z)
@@ -291,43 +281,37 @@
         come_sibling(m, 0).wait_recv()
         come_sibling(m, 1).wait_recv()
 
-        for h, first in ((0, 4), (1, 9)):
-            @pl.when(n == first)
+        @pl.when(n == 7)
+        def _():
+            side_terms_in.wait_recv()
+            turned[1 - x] = terms[1 - x].T
+
+        @pl.loop(0, 2)
+        def _(i):
+            late = 3 * (n - 7) - n // 11
+            late_stop = jnp.minimum(3 * (n - 6) - (n + 1) // 11, 12)
+            start = jnp.where(i == 1, n, jnp.where(n < 7, 0, late))
+            stop = jnp.where(i == 1, n + 1, jnp.where(n < 7, 0, late_stop))
+            group = jnp.where(i == 1, x, 1 - x)
+
+            def step(at, carry):
+                pool(at, group)
+                return carry
+
+            lax.fori_loop(start, stop, step, 0)
+
+            @pl.when(jnp.logical_and(n == 11, i == 0))
             def _():
-                side_terms_in(h).wait_recv()
-                if h == 0:
-                    side_terms(1).start()
-                turned[(1 - x) * 2 + h] = terms[(1 - x) * 2 + h].T
-
-        @pl.loop(0, 4)
-        def _(i):
-            late = 5 * (n - 9)
-            start = jnp.where(i == 1, jnp.where(n < 9, n, late), jnp.where(jnp.logical_and(i == 0, n == 4), 0, n))
-            late_stop = jnp.where(n < 9, n, jnp.minimum(late + 5, 12))
-            early_stop = jnp.where(jnp.logical_and(i == 0, n < 4), n, n + 1)
-            stop = jnp.where(i == 1, late_stop, early_stop)
-            q = jnp.where(i < 2, (1 - x) * 2 + i, x * 2 + i - 2)
-
-            def step(at, carry):
-                pool(at, q)
-                return carry
-
-            lax.fori_loop(start, stop, step, 0)
-
-            @pl.when(jnp.logical_and(n == 11, i < 2))
-            def _():
-                sums_to(i).start()
+                sums_to.start()
 
     row_32 = lax.broadcasted_iota(jnp.int32, (32, 128), 0)
     length_of = jnp.ones((32, 128), jnp.float32)
     for b in range(8):
         for j in range(3):
             length_of = jnp.where(row_32 == b % 2 * 16 + b // 2 * 4 + j, meta_all[b, 4 + j:5 + j, :], length_of)
-    length_wide = jnp.concatenate([length_of] * (CHUNK // 128), axis=1)
-    for h in range(2):
-        sums_to(h).wait_recv()
-        total = pooled[x * 2 + h] + sums_in[h]
-        doc_send[:, h * CHUNK:(h + 1) * CHUNK] = (total / length_wide).astype(jnp.bfloat16)
+    length_wide = jnp.concatenate([length_of] * 4, axis=1)
+    sums_to.wait_recv()
+    doc_send[...] = ((pooled[x] + sums_in[...]) / length_wide).astype(jnp.bfloat16)
 
     def doc_to(i):
         return send(doc_send, doc_all.at[d], doc_s.at[i], doc_r.at[d], (v, (d + i) % 8))
@@ -384,9 +368,8 @@
         part_to(i).start()
     part_all[v] = part_send[v]
 
-    for h in range(2):
-        side_terms(h).wait_send()
-        sums_to(h).wait_send()
+    side_terms.wait_send()
+    sums_to.wait_send()
 
     @pl.loop(0, 12)
     def _(m):
@@ -439,21 +422,21 @@
         out_specs=(vmem, vmem),
         scratch_shapes=[
             pltpu.VMEM((12, 256, width), jnp.bfloat16),
-            pltpu.VMEM((4, CHUNK, width), jnp.bfloat16),
-            pltpu.VMEM((4, width, CHUNK), jnp.bfloat16),
+            pltpu.VMEM((2, 512, width), jnp.bfloat16),
+            pltpu.VMEM((2, width, 512), jnp.bfloat16),
             pltpu.VMEM((128, 4096), jnp.bfloat16),
             pltpu.VMEM((8, 8, 128), jnp.float32),
             pltpu.VMEM((32, 4096), jnp.float32),
-            pltpu.VMEM((4, 32, CHUNK), jnp.float32),
+            pltpu.VMEM((2, 32, 512), jnp.float32),
             pltpu.VMEM((32, 512), jnp.bfloat16),
             pltpu.VMEM((8, 32, 512), jnp.bfloat16),
             pltpu.VMEM((32, 4096), jnp.bfloat16),
             pltpu.VMEM((32, 128), jnp.float32),
             pltpu.VMEM((4, 8, 128), jnp.float32),
             pltpu.VMEM((4, 8, 128), jnp.float32),
-            pltpu.VMEM((2, 32, CHUNK), jnp.float32),
-            dma(6), dma(2), dma(2), dma(24), dma(24), dma(24), dma(12), dma(12), dma(24), dma(24),
-            dma(8), dma(8), dma(8), dma(8), dma(4), dma(4), dma(2), dma(2),
+            pltpu.VMEM((32, 512), jnp.float32),
+            dma(5), dma(1), dma(1), dma(24), dma(24), dma(24), dma(12), dma(12), dma(24), dma(24),
+            dma(8), dma(8), dma(8), dma(8), dma(4), dma(4), dma(1), dma(1),
         ],
         compiler_params=pltpu.CompilerParams(
             collective_id=0, has_side_effects=True, vmem_limit_bytes=60 * 1024 * 1024

time: 99.6 us -> 97.4 us (0.978)
  Pallas kernels: 93.8 us -> 91.6 us
    pallas_call x1, Pallas kernels: 93.8 us -> 91.6 us  [local_kernel(): pl.pallas_call(head_kernel, out_shape=(jax.ShapeDtypeStruct((8, 4096), jn...]
where the time goes in v6:
time: 97.4 us; the launch traced here: 97.2 us
  Pallas kernels  91.6 us (94%)
  local copies, waits for them, and re-layouts  2.96 us (3%)
  other arithmetic  2.01 us (2%)
    pallas_call x1, Pallas kernels, local_kernel(): pl.pallas_call(head_kernel, out_shape=(jax.ShapeDtypeStruct((8, 4096), jn...  91.6 us

profile of v6, /device:TPU:0, one launch (start us, length us, event | category | flops | bytes accessed | tf_op | source)
XLA Modules:
  0.0 97.2 jit_solution(12706194527355175307)
XLA Ops:
  0.6 0.7 convert_element_type.18
  1.3 0.1 pad.6.clone
  1.4 0.1 pad.7.clone
  1.4 0.7 convert_bitcast_fusion
  2.1 0.7 fusion.meta
  2.8 91.6 %shard_map.68 = (f32[8,4096]{1,0:T(8,128)}, f32[8,128]{1,0:T(8,128)}) custom-call(bf16[3,64,2048]{2,1,0:T(8,128)(2,1)} %hidden.1, bf16[512,2048]{1,0:T(8,128)(2,1)} %weights.1, bf16[128,4096]{1,0:T(8,128)(2,1)} %queries.1, f32[8,128]{1,0:T(8,128)} %fusion.meta), custom_call_target="tpu_custom_call" | custom-call | tf_op jit(solution)/shard_map/pallas_call | solution.py:415
  94.4 1.5 %slice.12 = bf16[3,4096]{1,0:T(4,128)(2,1)} slice(f32[8,4096]{1,0:T(8,128)} %get-tuple-element.4), slice={[0:3], [0:4096]} | slice | bytes 49152 | tf_op jit(solution)/shard_map/slice | solution.py:445
  95.9 1.3 %reshape.13 = f32[6,128]{1,0:T(8,128)} reshape(f32[2,3,128]{2,1,0:T(4,128)} %bitcast.9) | data formatting | bytes 6144 | tf_op jit(solution)/shard_map/reshape | solution.py:446

commit v7 on v6

--- a/solution.py
+++ b/solution.py
@@ -216,27 +216,27 @@
 
     place = lax.broadcasted_iota(jnp.int32, (8, CHUNK), 0).astype(jnp.float32)
 
-    def pool(n, group):
-        zp, j = order(n)
-        m = zp * 3 + j
+    def pool(zp, group):
         for half in range(0, 512, CHUNK):
-            logits = jnp.dot(rows[m], turned[group, :, half:half + CHUNK], preferred_element_type=jnp.float32)
+            block = rows[pl.ds(zp * 3, 3)].reshape(768, rows.shape[2])
+            logits = jnp.dot(block, turned[group, :, half:half + CHUNK], preferred_element_type=jnp.float32)
             for core in range(2):
-                length = meta_all[2 * zp + core, pl.ds(4 + j, 1), :]
-                length = jnp.concatenate([length] * (CHUNK // 128), axis=1)
-                total = jnp.zeros((8, CHUNK), jnp.float32)
-                for side in range(2):
-                    room = length - place - (64 * x + 128 * side).astype(jnp.float32)
-                    at = 128 * core + 64 * side
-                    parts = [
-                        jnp.where(room > float(8 * i), jnp.maximum(logits[at + 8 * i:at + 8 * i + 8, :], 0.0), 0.0)
-                        for i in range(8)
-                    ]
-                    while len(parts) > 1:
-                        parts = [a + b + a * b for a, b in zip(parts[0::2], parts[1::2])]
-                    total = total + jnp.log1p(parts[0])
-                row = pl.ds(core * 16 + zp * 4 + j, 1)
-                pooled[group, row, half:half + CHUNK] = jnp.sum(total, axis=0, keepdims=True)
+                for j in range(3):
+                    length = meta_all[2 * zp + core, 4 + j:5 + j, :]
+                    length = jnp.concatenate([length] * (CHUNK // 128), axis=1)
+                    total = jnp.zeros((8, CHUNK), jnp.float32)
+                    for side in range(2):
+                        room = length - place - (64 * x + 128 * side).astype(jnp.float32)
+                        at = 256 * j + 128 * core + 64 * side
+                        parts = [
+                            jnp.where(room > float(8 * i), jnp.maximum(logits[at + 8 * i:at + 8 * i + 8, :], 0.0), 0.0)
+                            for i in range(8)
+                        ]
+                        while len(parts) > 1:
+                            parts = [a + b + a * b for a, b in zip(parts[0::2], parts[1::2])]
+                        total = total + jnp.log1p(parts[0])
+                    row = pl.ds(core * 16 + zp * 4 + j, 1)
+                    pooled[group, row, half:half + CHUNK] = jnp.sum(total, axis=0, keepdims=True)
 
     sums_to = send(pooled.at[1 - x], sums_in, sum_s.at[0], sum_r.at[0], x_side)
 
@@ -288,17 +288,18 @@
 
         @pl.loop(0, 2)
         def _(i):
-            late = 3 * (n - 7) - n // 11
-            late_stop = jnp.minimum(3 * (n - 6) - (n + 1) // 11, 12)
-            start = jnp.where(i == 1, n, jnp.where(n < 7, 0, late))
-            stop = jnp.where(i == 1, n + 1, jnp.where(n < 7, 0, late_stop))
+            turn = jnp.where(i == 1, n, jnp.where(n < 7, 0, jnp.where(n == 7, 2, jnp.where(n == 8, 5, jnp.where(n == 11, 11, n - 1)))))
+            at_end = jnp.where(z == 0, turn // 3, 3 - turn // 3)
+            at_mid = jnp.where(turn == 2, z, jnp.where(turn == 8, z - 1, jnp.where(turn == 9, z + 1, jnp.where(z == 1, 3, 0))))
+            end = jnp.logical_or(z == 0, z == 3)
+            due_end = turn % 3 == 2
+            due_mid = jnp.logical_or(jnp.logical_or(turn == 2, turn == 8), jnp.logical_or(turn == 9, turn == 11))
+            due = jnp.where(end, due_end, due_mid)
             group = jnp.where(i == 1, x, 1 - x)
 
-            def step(at, carry):
-                pool(at, group)
-                return carry
-
-            lax.fori_loop(start, stop, step, 0)
+            @pl.when(due)
+            def _():
+                pool(jnp.where(end, at_end, at_mid), group)
 
             @pl.when(jnp.logical_and(n == 11, i == 0))
             def _():

time: 97.4 us -> 96.6 us (level)
  no operation moved by 1% of the time
where the time goes in v7:
time: 96.6 us; the launch traced here: 96.4 us
  Pallas kernels  90.8 us (94%)
  local copies, waits for them, and re-layouts  2.96 us (3%)
  other arithmetic  2.01 us (2%)
    pallas_call x1, Pallas kernels, local_kernel(): pl.pallas_call(head_kernel, out_shape=(jax.ShapeDtypeStruct((8, 4096), jn...  90.8 us

profile of v7, /device:TPU:0, one launch (start us, length us, event | category | flops | bytes accessed | tf_op | source)
XLA Modules:
  0.0 96.4 jit_solution(433714973585033395)
XLA Ops:
  0.6 0.7 convert_element_type.18
  1.3 0.1 pad.6.clone
  1.4 0.1 pad.7.clone
  1.4 0.7 convert_bitcast_fusion
  2.1 0.7 fusion.meta
  2.8 90.8 %shard_map.68 = (f32[8,4096]{1,0:T(8,128)}, f32[8,128]{1,0:T(8,128)}) custom-call(bf16[3,64,2048]{2,1,0:T(8,128)(2,1)} %hidden.1, bf16[512,2048]{1,0:T(8,128)(2,1)} %weights.1, bf16[128,4096]{1,0:T(8,128)(2,1)} %queries.1, f32[8,128]{1,0:T(8,128)} %fusion.meta), custom_call_target="tpu_custom_call" | custom-call | tf_op jit(solution)/shard_map/pallas_call | solution.py:416
  93.6 1.5 %slice.12 = bf16[3,4096]{1,0:T(4,128)(2,1)} slice(f32[8,4096]{1,0:T(8,128)} %get-tuple-element.4), slice={[0:3], [0:4096]} | slice | bytes 49152 | tf_op jit(solution)/shard_map/slice | solution.py:446
  95.1 1.3 %reshape.13 = f32[6,128]{1,0:T(8,128)} reshape(f32[2,3,128]{2,1,0:T(4,128)} %bitcast.9) | data formatting | bytes 6144 | tf_op jit(solution)/shard_map/reshape | solution.py:447
